TPU v7x, 32 devices: a whole 2x2x4 slice. The times are simulated.
32 devices in a mesh: seq: 16 (over z, y, x), head: 2 (over core).
Axes of the slice: x: 2, y: 2, z: 4, core: 2. Of those that a mesh axis runs over, the one named last changes fastest.
Arguments:
- queries: bfloat16 [8192, 4096], P('seq', 'head'), may hold values from -6 to 6
- keys: bfloat16 [8192, 4096], P('seq', 'head'), may hold values from -6 to 6
- values: bfloat16 [8192, 4096], P('seq', 'head')
- gain: float32 [4096], P('head'), may hold values from 0.1 to 1.9
- cotangent: bfloat16 [8192, 4096], P('seq', 'head')
- doc_lengths: int32 [16], replicated, may hold values from 1 to 4096, 8192 in all
Outputs:
- attended: bfloat16 [8192, 4096], P('seq', 'head')
- grad_queries: bfloat16 [8192, 4096], P('seq', 'head')
- grad_keys: bfloat16 [8192, 4096], P('seq', 'head')
- grad_values: bfloat16 [8192, 4096], P('seq', 'head')
Inputs may be any that keep to these rules, and one draw needn't show every extreme that they name: `doc_lengths`: the lengths sum to 8192; the longest document has exactly 4096 tokens.
All inputs are finite; a program needn't handle non-finite values.
Results may differ from a plain program's by a relative error of at most 0.0059.
Values sent between devices are 32-bit elements; how exact they have to be, the bound alone decides.
A program may use at most 192 MiB of HBM per device.

v0:
```python
import jax
import jax.numpy as jnp
from jax import lax
from jax.sharding import PartitionSpec as P

DH = 128
HEADS = 32


epsilon = 1e-05


def carried_in(value, axis, join, neutral, backward):
    count, mine = (lax.axis_size(axis), lax.axis_index(axis))
    pieces = jax.tree.map(lambda part: lax.all_gather(part, axis), value)
    if backward:
        pieces = jax.tree.map(lambda part: part[::-1], pieces)
        mine = count - 1 - mine
    subtotal = jax.tree.map(
        lambda part, zero: jnp.full_like(part, 0) + jnp.asarray(zero, part.dtype), value, neutral
    )

    def step(position, subtotal):
        longer = join(subtotal, jax.tree.map(lambda part: part[position], pieces))
        return jax.tree.map(lambda new, old: jnp.where(position < mine, new, old), longer, subtotal)

    return lax.fori_loop(0, count - 1, step, subtotal)


def doc_index(starts, positions):
    return jnp.sum((starts[None, :] <= positions[:, None]).astype(jnp.int32), axis=1)


def compose(earlier, later):
    return (later[0] + later[1] * earlier[0], later[1] * earlier[1])


def on_device(queries, keys, values, gain, cotangent, doc_lengths):
    tokens = queries.shape[0]
    heads_here = queries.shape[1] // DH
    model_width = HEADS * DH
    query_row_list = queries.reshape(tokens, heads_here, DH)
    key_row_list = keys.reshape(tokens, heads_here, DH)
    value_row_list = values.reshape(tokens, heads_here, DH)
    starts = jnp.cumsum(doc_lengths) - doc_lengths
    anchor = lax.axis_index("seq") * tokens
    positions = anchor + jnp.arange(tokens, dtype=jnp.int32)
    doc_ids = doc_index(starts, positions)
    bounds = jnp.stack([anchor - 1, anchor, anchor + tokens - 1, anchor + tokens])
    edge_docs = doc_index(starts, bounds)
    offsets = jnp.arange(tokens, dtype=jnp.int32)
    visible = ((doc_ids[:, None] == doc_ids[None, :]) & (offsets[:, None] >= offsets[None, :]))[
        None
    ]
    entering_state = (doc_ids == edge_docs[0])[:, None, None]
    opening_boundary = (doc_ids == edge_docs[1])[:, None, None]
    closing_boundary = (doc_ids == edge_docs[2])[:, None, None]
    leaving_state = (doc_ids == edge_docs[3])[:, None, None]
    scores = jnp.einsum(
        "thk,shk->hts", query_row_list, key_row_list, preferred_element_type=jnp.float32
    )
    weights = jnp.where(visible, scores, 0.0).astype(jnp.bfloat16)
    inside_state = jnp.einsum(
        "blp,blq->lpq",
        jnp.where(closing_boundary, key_row_list, jnp.zeros_like(key_row_list)),
        value_row_list,
        preferred_element_type=jnp.float32,
    )
    keep_forward = (edge_docs[2] == edge_docs[0]).astype(jnp.float32)
    start_pair = (jnp.zeros_like(inside_state), jnp.ones_like(keep_forward))
    carried = carried_in((inside_state, keep_forward), "seq", compose, start_pair, False)[0]
    carried_narrow_state = carried.astype(jnp.bfloat16)
    output_rows = jnp.einsum(
        "hts,shv->thv", weights, value_row_list, preferred_element_type=jnp.float32
    )
    output_rows = output_rows + jnp.where(
        entering_state,
        jnp.einsum(
            "ldi,dir->ldr", query_row_list, carried_narrow_state, preferred_element_type=jnp.float32
        ),
        0.0,
    )
    flat_out = output_rows.reshape(tokens, heads_here * DH)
    scaled_grad = cotangent.astype(jnp.float32) * gain
    square_sum, cross_sum = lax.psum(
        (jnp.sum(flat_out * flat_out, axis=1), jnp.sum(scaled_grad * flat_out, axis=1)), "head"
    )
    root_mean = jnp.sqrt(square_sum / model_width + epsilon)
    attended = (flat_out / root_mean[:, None] * gain).astype(jnp.bfloat16)
    coefficient = cross_sum / (model_width * root_mean * root_mean)
    grad_out = ((scaled_grad - flat_out * coefficient[:, None]) / root_mean[:, None]).astype(
        jnp.bfloat16
    )
    gradient_row_list = grad_out.reshape(tokens, heads_here, DH)
    back_scores = jnp.einsum(
        "thv,shv->hts", gradient_row_list, value_row_list, preferred_element_type=jnp.float32
    )
    back_weights = jnp.where(visible, back_scores, 0.0).astype(jnp.bfloat16)
    inside_backward_state = jnp.einsum(
        "dmi,dmc->mic",
        jnp.where(opening_boundary, query_row_list, jnp.zeros_like(query_row_list)),
        gradient_row_list,
        preferred_element_type=jnp.float32,
    )
    keep_backward = (edge_docs[3] == edge_docs[1]).astype(jnp.float32)
    back_pair = (jnp.zeros_like(inside_backward_state), jnp.ones_like(keep_backward))
    later_state = carried_in(
        (inside_backward_state, keep_backward), "seq", compose, back_pair, True
    )[0]
    following_narrow = later_state.astype(jnp.bfloat16)
    gradient_query = jnp.einsum(
        "hts,shk->thk", back_weights, key_row_list, preferred_element_type=jnp.float32
    )
    gradient_query = gradient_query + jnp.where(
        entering_state,
        jnp.einsum(
            "esn,son->eso",
            gradient_row_list,
            carried_narrow_state,
            preferred_element_type=jnp.float32,
        ),
        0.0,
    )
    gradient_key = jnp.einsum(
        "hts,thk->shk", back_weights, query_row_list, preferred_element_type=jnp.float32
    )
    gradient_key = gradient_key + jnp.where(
        leaving_state,
        jnp.einsum(
            "won,ozn->woz", value_row_list, following_narrow, preferred_element_type=jnp.float32
        ),
        0.0,
    )
    gradient_value = jnp.einsum(
        "hts,thv->shv", weights, gradient_row_list, preferred_element_type=jnp.float32
    )
    gradient_value = gradient_value + jnp.where(
        leaving_state,
        jnp.einsum(
            "xua,uat->xut", key_row_list, following_narrow, preferred_element_type=jnp.float32
        ),
        0.0,
    )
    flat_shape = (tokens, heads_here * DH)
    return (
        attended,
        gradient_query.reshape(flat_shape).astype(jnp.bfloat16),
        gradient_key.reshape(flat_shape).astype(jnp.bfloat16),
        gradient_value.reshape(flat_shape).astype(jnp.bfloat16),
    )


def solution(mesh):
    placed = (
        P("seq", "head"),
        P("seq", "head"),
        P("seq", "head"),
        P("head"),
        P("seq", "head"),
        P(),
    )
    return jax.shard_map(
        on_device,
        mesh=mesh,
        in_specs=placed,
        out_specs=(P("seq", "head"), P("seq", "head"), P("seq", "head"), P("seq", "head")),
        check_vma=False,
    )
```

profile of v0, /device:TPU:0, one launch (start us, length us, event | category | flops | bytes accessed | tf_op | source)
XLA Modules:
  0.0 581.0 jit_solution(6208078079081330287)
XLA Ops:
  7.2 0.9 copy.85
  9.9 3.5 copy.116
  13.4 4.3 copy.89
  17.7 2.5 broadcast_compare_fusion.1
  20.2 3.3 fusion.9
  26.2 3.9 copy.112
  31.5 0.7 dynamic-update-slice
  32.2 44.5 %all-reduce.2 = (f32[16]{0:T(128)S(1)}, f32[16]{0:T(128)S(1)}) all-reduce(f32[16]{0:T(128)S(1)} %dynamic-update-slice, f32[16]{0:T(128)S(1)} %dynamic-update-slice.1), channel_id=1, replica_groups=mesh['seq'=16,'head'=2] {'seq'}, use_global_device_ids=true, to_apply=%add | all-reduce | flops 32 | bytes 256
  76.9 4.7 select_convert_fusion.1
  81.7 3.2 copy-done.1
  84.9 4.8 fusion.4
  89.7 128.9 %all-gather.5.cloned.1.call-done = f32[256,128,128]{2,1,0:T(8,128)} async-done(((f32[16,128,128]{2,1,0:T(8,128)}), f32[256,128,128]{2,1,0:T(8,128)}) %all-gather.5.cloned.1.call-update) | async-done | bytes 16777232 | tf_op jit(solution)/shard_map/all_gather | solution.py:15
  218.6 50.8 %while.28 = (s32[]{:T(128)}, f32[16,128,128]{2,1,0:T(8,128)S(1)}, s32[]{:T(128)}, f32[16,16,128,128]{3,2,1,0:T(8,128)}, f32[16]{0:T(128)S(1)}, /*index=5*/s32[]{:T(128)}, s32[]{:T(128)}) while((s32[]{:T(128)}, f32[16,128,128]{2,1,0:T(8,128)S(1)}, s32[]{:T(128)}, f32[16,16,128,128]{3,2,1,0:T(8,128)}, f32[16]{0:T(128)S(1)}, ...), condition=%wide.region_4.5_spmd.clone, body=%wide.region_3.4_spmd.clone.sunk | while | flops 1048580 | bytes 3145853 | solution.py:27
  219.2 2.8 fusion.57
  222.6 2.8 fusion.57
  226.0 2.8 fusion.57
  229.4 2.8 fusion.57
  232.8 2.8 fusion.57
  236.2 2.8 fusion.57
  239.6 2.8 fusion.57
  242.9 2.8 fusion.57
  246.3 2.8 fusion.57
  249.7 2.8 fusion.57
  253.1 2.8 fusion.57
  256.5 2.8 fusion.57
  259.9 2.8 fusion.57
  263.3 2.8 fusion.57
  266.7 2.8 fusion.57
  269.5 5.6 multiply_reduce_fusion.1
  275.0 5.5 copy.93
  280.5 3.5 multiply_reduce_fusion
  284.0 2.6 all-reduce.3
  286.6 4.9 divide_convert_fusion
  291.5 3.9 copy.113
  295.5 3.9 fusion.13
  299.5 4.2 select_convert_fusion
  303.8 4.8 fusion.35
  309.2 4.3 fusion.3
  313.5 3.9 copy.107
  317.4 7.2 %fusion.36 = f32[16,128,512]{2,1,0:T(8,128)} fusion(bf16[512,16,128]{0,2,1:T(8,128)(2,1)} %bitcast.106, bf16[16,512,512]{2,1,0:T(8,128)(2,1)} %copy-done.1), kind=kOutput, calls=%fused_computation.60 | convolution fusion | flops 1073741824 | bytes 14680064 | tf_op jit(solution)/shard_map/hts,thv->shv/dot_general | solution.py:134
  324.7 164.7 %all-gather.7.cloned.1.call-done = f32[256,128,128]{2,1,0:T(8,128)} async-done(((f32[16,128,128]{2,1,0:T(8,128)}), f32[256,128,128]{2,1,0:T(8,128)}) %all-gather.7.cloned.1.call-update) | async-done | bytes 16777232 | tf_op jit(solution)/shard_map/all_gather | solution.py:15
  489.4 11.7 %rev.6 = f32[16,16,128,128]{3,2,1,0:T(8,128)} reverse(f32[16,16,128,128]{3,2,1,0:T(8,128)} %bitcast.112), dimensions={0} | reverse | bytes 33554432 | tf_op jit(solution)/shard_map/rev | solution.py:17
  501.1 50.8 %while.29 = (s32[]{:T(128)}, f32[16,128,128]{2,1,0:T(8,128)S(1)}, s32[]{:T(128)}, f32[16,16,128,128]{3,2,1,0:T(8,128)}, f32[16]{0:T(128)S(1)}, /*index=5*/s32[]{:T(128)}, s32[]{:T(128)}) while((s32[]{:T(128)}, f32[16,128,128]{2,1,0:T(8,128)S(1)}, s32[]{:T(128)}, f32[16,16,128,128]{3,2,1,0:T(8,128)}, f32[16]{0:T(128)S(1)}, ...), condition=%wide.region_10.11_spmd.clone, body=%wide.region_9.10_spmd.clone.sunk | while | flops 1048580 | bytes 3145853 | solution.py:27
  501.6 2.8 fusion.58
  505.0 2.8 fusion.58
  508.4 2.8 fusion.58
  511.8 2.8 fusion.58
  515.2 2.8 fusion.58
  518.6 2.8 fusion.58
  522.0 2.8 fusion.58
  525.4 2.8 fusion.58
  528.8 2.8 fusion.58
  532.1 2.8 fusion.58
  535.5 2.8 fusion.58
  538.9 2.8 fusion.58
  542.3 2.8 fusion.58
  545.7 2.8 fusion.58
  549.1 2.8 fusion.58
  551.9 2.9 fusion.6
  555.3 0.9 copy-done.6
  556.3 2.3 add_convert_fusion
  558.5 3.9 copy.109
  562.4 7.8 %fusion.2 = bf16[512,16,128]{0,2,1:T(8,128)(2,1)} fusion(f32[16,128,512]{2,1,0:T(8,128)} %fusion.6, bf16[512,16,128]{0,2,1:T(8,128)(2,1)} %bitcast.111, bf16[16,512,512]{2,1,0:T(8,128)(2,1)} %copy-done.3, pred[512]{0:T(512)(128)(4,1)S(1)} %get-tuple-element.272), kind=kOutput, calls=%fused_computation.7 | convolution fusion | flops 1076887552 | bytes 16777728 | tf_op jit(solution)/shard_map/hts,thk->shk/dot_general | solution.py:124
  570.2 3.9 copy.108
  (69 shorter events, 22.4 us)
Async XLA Ops:
  7.2 13.1 %copy-start = (bf16[512,2048]{1,0:T(8,128)(2,1)S(1)}, bf16[512,2048]{1,0:T(8,128)(2,1)}, u32[]{:S(2)}) copy-start(bf16[512,2048]{1,0:T(8,128)(2,1)} %param.12) | copy-start | bytes 6291460
  7.2 211.5 %all-gather.5.cloned.1.call-start = ((), (), s32[]{:S(2)}) async-start(), calls=%async_computation | async-start | bytes 17825792 | tf_op jit(solution)/shard_map/all_gather | solution.py:15
  23.6 465.8 %all-gather.7.cloned.1.call-start = ((), (), s32[]{:S(2)}) async-start(), calls=%async_computation.1 | async-start | bytes 17825792 | tf_op jit(solution)/shard_map/all_gather | solution.py:15
  26.2 3.9 copy-start.9
  81.7 3.2 copy-start.1
  275.0 5.5 copy-start.8
  299.5 4.3 copy-start.7
  303.8 5.4 copy-start.3
  303.8 5.4 copy-start.5
  489.4 11.7 %copy-start.2 = (f32[16,128,128]{2,1,0:T(8,128)S(1)}, f32[16,128,128]{2,1,0:T(8,128)}, u32[]{:S(2)}) copy-start(f32[16,128,128]{2,1,0:T(8,128)} %custom-call.1) | copy-start | bytes 3145732
  551.9 3.4 copy-start.4
  551.9 4.4 copy-start.6
Sparse Core Ops, SparseCore 0:
  23.7 194.9 all-gather.4
  299.5 189.7 all-gather.6
where the time goes:
time: 583 us; the launch traced here: 581 us
  waiting for transfers between devices  294 us (50%)
  other arithmetic  95.6 us (16%)
  local copies, waits for them, and re-layouts  71.2 us (12%)
  matrix products  55.8 us (10%)
  blocking collectives  47.2 us (8%)
  between operations  16.7 us (3%)
    all_gather x2, waiting for transfers between devices, carried_in(): pieces = jax.tree.map(lambda part: lax.all_gather(part, axis), value)  294 us
    select_n x30, other arithmetic, step(): jnp.where(position < mine, new, old)  83.4 us
    unnamed x1, blocking collectives  44.5 us
    unnamed x29, local copies, waits for them, and re-layouts  22.8 us
    dynamic_slice x30, local copies, waits for them, and re-layouts, step(): longer = join(subtotal, jax.tree.map(lambda part: part[position], pieces))  17.6 us
    rev x2, local copies, waits for them, and re-layouts, carried_in(): pieces = jax.tree.map(lambda part: part[::-1], pieces)  11.8 us
  transfers between devices with their start and end apart: 2, of which 2 were waited for; matrix products, arithmetic and copies ran while one was open for 7% of the time, Pallas kernels for 0%

commit v1 on v0

v1 whole, which is shorter than its diff:
```python
import functools

import jax
import jax.numpy as jnp
from jax import lax
from jax.experimental import pallas as pl
from jax.experimental.pallas import tpu as pltpu
from jax.sharding import PartitionSpec as P

DH = 128
HEADS = 32
QUAD = 4

epsilon = 1e-05
MESH = pl.DeviceIdType.MESH
F32 = jnp.float32
BF16 = jnp.bfloat16


def nn(a, b):
    return lax.dot_general(a, b, (((1,), (0,)), ((), ())), preferred_element_type=F32)


def nt(a, b):
    return lax.dot_general(a, b, (((1,), (1,)), ((), ())), preferred_element_type=F32)


def tn(a, b):
    return lax.dot_general(a, b, (((0,), (0,)), ((), ())), preferred_element_type=F32)


def pick(flag, one, other):
    return jnp.where(flag, one, other).astype(F32)


def equal(a, b):
    return jnp.where(a == b, 1.0, 0.0).astype(F32)


def kernel(
    n, nh, docs,
    lens, q, k, v, gain, cot,
    att, gq, gk, gv,
    wts, out, gks, grad, carr,
    vis, ment, mopen, mclose, mleave, part, peer,
    loc_f, pair_f, chain_f, rx_f, ry_f, rz_f,
    loc_b, pair_b, chain_b, rx_b, ry_b, rz_b,
    sx_f, sy_f, sz_f, tx_f, ty_f, tz_f,
    sx_b, sy_b, sz_b, tx_b, ty_b, tz_b,
    sh, th,
):
    tokens = q.shape[0]
    half = tokens // 2
    heads = q.shape[1] // DH
    width = float(HEADS * DH)
    me = lax.axis_index("seq")
    mine = lax.axis_index("head")
    odd = lax.rem(me, 2)
    zc = lax.div(me, QUAD)
    nz = n // QUAD
    q0 = zc * QUAD
    upper = lax.div(me - q0, 2)
    pb = me - odd
    px = me + 1 - 2 * odd
    py = me + 2 - 4 * upper
    up = lax.rem(me + QUAD, n)
    down = lax.rem(me + n - QUAD, n)

    barrier = pltpu.get_barrier_semaphore()
    pl.semaphore_signal(barrier, inc=1, device_id={"seq": px}, device_id_type=MESH)
    pl.semaphore_signal(barrier, inc=1, device_id={"seq": py}, device_id_type=MESH)

    @pl.when(zc < nz - 1)
    def _():
        pl.semaphore_signal(barrier, inc=1, device_id={"seq": up}, device_id_type=MESH)

    @pl.when(zc > 0)
    def _():
        pl.semaphore_signal(barrier, inc=1, device_id={"seq": down}, device_id_type=MESH)

    for d in range(1, nh):
        pl.semaphore_signal(
            barrier, inc=1, device_id={"head": lax.rem(mine + d, nh)}, device_id_type=MESH
        )

    starts = []
    total = jnp.int32(0)
    for i in range(docs):
        starts.append(total)
        total = total + lens[i]

    def doc_of(p):
        count = jnp.int32(0)
        for s in starts:
            count = count + jnp.where(s <= p, 1, 0).astype(jnp.int32)
        return count

    before = {}
    after = {}
    for name, i in (("q0", q0), ("q2", q0 + 2), ("q4", q0 + 4), ("pb", pb), ("p1", pb + 1),
                    ("p2", pb + 2), ("me", me), ("m1", me + 1)):
        before[name] = doc_of(i * tokens - 1)
        after[name] = doc_of(i * tokens)

    anchor = me * tokens
    pos_c = lax.broadcasted_iota(jnp.int32, (tokens, DH), 0) + anchor
    doc_c = jnp.zeros((tokens, DH), jnp.int32)
    for s in starts:
        doc_c = doc_c + jnp.where(pos_c >= s, 1, 0)
    ment[...] = jnp.where(doc_c == before["me"], 1.0, 0.0).astype(BF16)
    mopen[...] = jnp.where(doc_c == after["me"], 1.0, 0.0).astype(BF16)
    mclose[...] = jnp.where(doc_c == before["m1"], 1.0, 0.0).astype(BF16)
    mleave[...] = jnp.where(doc_c == after["m1"], 1.0, 0.0).astype(BF16)

    pl.semaphore_wait(
        barrier,
        2 + nh - 1
        + jnp.where(zc < nz - 1, 1, 0).astype(jnp.int32)
        + jnp.where(zc > 0, 1, 0).astype(jnp.int32),
    )

    def cols(h):
        return pl.ds(pl.multiple_of(h * DH, DH), DH)

    def send(src, dst, ss, rs, h, to):
        return pltpu.make_async_remote_copy(
            src_ref=src.at[h], dst_ref=dst.at[h], send_sem=ss.at[h], recv_sem=rs.at[h],
            device_id={"seq": to}, device_id_type=MESH,
        )

    class Scan:
        def __init__(self, bufs, sems, to, place, coef):
            self.loc, self.pair, self.chain, self.rx, self.ry, self.rz = bufs
            self.sx, self.sy, self.sz, self.tx, self.ty, self.tz = sems
            self.to, self.place = to, place
            self.al, self.ar, self.er, self.bl, self.br, self.e2, self.kq, self.e3 = coef

        def cx(self, h):
            return send(self.loc, self.rx, self.sx, self.tx, h, px)

        def cy(self, h):
            return send(self.pair, self.ry, self.sy, self.ty, h, py)

        def cz(self, h):
            return send(self.chain, self.rz, self.sz, self.tz, h, self.to)

        def clear(self):
            @pl.when(self.place == 0)
            def _():
                self.rz[...] = jnp.zeros_like(self.rz)

        def xstage(self, h):
            self.cx(h).wait_recv()
            self.pair[h] = self.al * self.loc[h] + self.ar * self.rx[h]
            self.cy(h).start()

        def ystage(self, h):
            self.cy(h).wait_recv()

            @pl.when(self.place == 0)
            def _():
                self.chain[h] = self.bl * self.pair[h] + self.br * self.ry[h]
                self.cz(h).start()

        def zstage(self, h):
            @pl.when(self.place > 0)
            def _():
                self.cz(h).wait_recv()

            @pl.when((self.place > 0) & (self.place < nz - 1))
            def _():
                total = self.bl * self.pair[h] + self.br * self.ry[h]
                self.chain[h] = total + self.kq * self.rz[h]
                self.cz(h).start()

            return self.er * self.rx[h] + self.e2 * self.ry[h] + self.e3 * self.rz[h]

        def drain(self):
            def body(h, carry):
                self.cx(h).wait_send()
                self.cy(h).wait_send()

                @pl.when(self.place < nz - 1)
                def _():
                    self.cz(h).wait_send()

                return carry

            lax.fori_loop(0, heads, body, 0)

    is_odd, is_upper = odd == 1, upper == 1
    kx = equal(before["p1"], before["p2"])
    ky = equal(before["q2"], before["q4"])
    fwd = Scan(
        (loc_f, pair_f, chain_f, rx_f, ry_f, rz_f),
        (sx_f, sy_f, sz_f, tx_f, ty_f, tz_f),
        up, zc,
        (pick(is_odd, 1.0, kx), pick(is_odd, kx, 1.0), pick(is_odd, 1.0, 0.0),
         pick(is_upper, 1.0, ky), pick(is_upper, ky, 1.0),
         pick(is_upper, equal(before["pb"], before["me"]), 0.0),
         equal(before["q0"], before["q4"]), equal(before["q0"], before["me"])),
    )
    kx = equal(after["pb"], after["p1"])
    ky = equal(after["q0"], after["q2"])
    bwd = Scan(
        (loc_b, pair_b, chain_b, rx_b, ry_b, rz_b),
        (sx_b, sy_b, sz_b, tx_b, ty_b, tz_b),
        down, nz - 1 - zc,
        (pick(is_odd, kx, 1.0), pick(is_odd, 1.0, kx), pick(is_odd, 0.0, 1.0),
         pick(is_upper, ky, 1.0), pick(is_upper, 1.0, ky),
         pick(is_upper, 0.0, equal(after["m1"], after["p2"])),
         equal(after["q0"], after["q4"]), equal(after["m1"], after["q4"])),
    )

    def slots(scan, inside, finish):
        def place_of(s):
            return s - 1 - 2 * scan.place

        def chain_step(s):
            h = place_of(s)

            @pl.when((h >= 0) & (h < heads))
            def _():
                finish(h, scan.zstage(h).astype(BF16))

        def main(s, carry):
            scan.xstage(s)

            @pl.when(s > 0)
            def _():
                scan.ystage(s - 1)

            inside(s)
            chain_step(s)
            return carry

        lax.fori_loop(0, heads, main, 0)
        scan.ystage(heads - 1)

        def tail(s, carry):
            chain_step(s)
            return carry

        lax.fori_loop(heads, heads + 1 + 2 * (nz - 1), tail, 0)

    def first(h, carry):
        c = cols(h)
        loc_f[h] = tn(k[:, c] * mclose[...], v[:, c])
        fwd.cx(h).start()
        return carry

    lax.fori_loop(0, heads, first, 0)
    fwd.clear()
    bwd.clear()

    pos_r = lax.broadcasted_iota(jnp.int32, (8, tokens), 1) + anchor
    doc_r = jnp.zeros((8, tokens), jnp.int32)
    for s in starts:
        doc_r = doc_r + jnp.where(pos_r >= s, 1, 0)
    row = lax.broadcasted_iota(jnp.int32, (tokens, tokens), 0)
    col = lax.broadcasted_iota(jnp.int32, (tokens, tokens), 1)
    vis[...] = jnp.where((doc_c[:, :1] == doc_r[:1, :]) & (row >= col), 1, 0)
    part[...] = jnp.zeros_like(part)

    lo, hi = slice(0, half), slice(half, tokens)

    def masked(scores, rows, columns):
        return jnp.where(vis[rows, columns] != 0, scores, 0.0).astype(BF16)

    def inside_f(h):
        c = cols(h)
        w0 = masked(nt(q[lo, c], k[lo, c]), lo, lo)
        w1 = masked(nt(q[hi, c], k[:, c]), hi, slice(0, tokens))
        wts[h, lo, lo] = w0
        wts[h, hi, :] = w1
        out[lo, c] = nn(w0, v[lo, c])
        out[hi, c] = nn(w1, v[:, c])

    def finish_f(h, low):
        c = cols(h)
        carr[h] = low
        o = out[:, c] + nn(q[:, c] * ment[...], low)
        out[:, c] = o
        part[0] += o * o
        part[1] += (cot[:, c].astype(F32) * gain[:, c]) * o

    slots(fwd, inside_f, finish_f)

    def swap(d):
        return pltpu.make_async_remote_copy(
            src_ref=part, dst_ref=peer.at[d - 1], send_sem=sh.at[d - 1], recv_sem=th.at[d - 1],
            device_id={"head": lax.rem(mine + d, nh)}, device_id_type=MESH,
        )

    for d in range(1, nh):
        swap(d).start()
    for d in range(1, nh):
        swap(d).wait_recv()
    squares, cross = part[0], part[1]
    for d in range(1, nh):
        squares = squares + peer[d - 1, 0]
        cross = cross + peer[d - 1, 1]
    for d in range(1, nh):
        swap(d).wait_send()
    root = jnp.sqrt(jnp.sum(squares, axis=1, keepdims=True) / width + epsilon)
    coef = jnp.sum(cross, axis=1, keepdims=True) / (width * root * root)
    part[0] = jnp.broadcast_to(1.0 / root, (tokens, DH))
    part[1] = jnp.broadcast_to(coef, (tokens, DH))

    def middle(h, carry):
        c = cols(h)
        o = out[:, c]
        inv = part[0]
        gn = gain[:, c]
        att[:, c] = (o * inv * gn).astype(BF16)
        g = ((cot[:, c].astype(F32) * gn - o * part[1]) * inv).astype(BF16)
        grad[:, c] = g
        loc_b[h] = tn(q[:, c] * mopen[...], g)
        bwd.cx(h).start()
        return carry

    lax.fori_loop(0, heads, middle, 0)

    def inside_b(h):
        c = cols(h)
        b0 = masked(nt(grad[lo, c], v[lo, c]), lo, lo)
        b1 = masked(nt(grad[hi, c], v[:, c]), hi, slice(0, tokens))
        entering = nt(grad[:, c] * ment[...], carr[h])
        gq[lo, c] = (nn(b0, k[lo, c]) + entering[lo]).astype(BF16)
        gq[hi, c] = (nn(b1, k[:, c]) + entering[hi]).astype(BF16)
        gks[lo, c] = tn(b0, q[lo, c]) + tn(b1[:, lo], q[hi, c])
        gks[hi, c] = tn(b1[:, hi], q[hi, c])
        w1 = wts[h, hi, :]
        out[lo, c] = tn(wts[h, lo, lo], grad[lo, c]) + tn(w1[:, lo], grad[hi, c])
        out[hi, c] = tn(w1[:, hi], grad[hi, c])

    def finish_b(h, low):
        c = cols(h)
        gk[:, c] = (gks[:, c] + nt(v[:, c] * mleave[...], low)).astype(BF16)
        gv[:, c] = (out[:, c] + nn(k[:, c] * mleave[...], low)).astype(BF16)

    slots(bwd, inside_b, finish_b)
    fwd.drain()
    bwd.drain()


def on_device(n, nh, queries, keys, values, gain, cotangent, doc_lengths):
    tokens, wide = queries.shape
    heads = wide // DH
    vmem = pl.BlockSpec(memory_space=pltpu.VMEM)
    state = pltpu.VMEM((heads, DH, DH), F32)
    sems = pltpu.SemaphoreType.DMA((heads,))
    low = pltpu.VMEM((tokens, DH), BF16)
    shape = jax.ShapeDtypeStruct((tokens, wide), BF16)
    return pl.pallas_call(
        functools.partial(kernel, n, nh, doc_lengths.shape[0]),
        out_shape=(shape,) * 4,
        in_specs=[pl.BlockSpec(memory_space=pltpu.SMEM)] + [vmem] * 5,
        out_specs=(vmem,) * 4,
        scratch_shapes=[
            pltpu.VMEM((heads, tokens, tokens), BF16),
            pltpu.VMEM((tokens, wide), F32),
            pltpu.VMEM((tokens, wide), F32),
            pltpu.VMEM((tokens, wide), BF16),
            pltpu.VMEM((heads, DH, DH), BF16),
            pltpu.VMEM((tokens, tokens), jnp.int32),
            low, low, low, low,
            pltpu.VMEM((2, tokens, DH), F32),
            pltpu.VMEM((nh - 1, 2, tokens, DH), F32),
        ]
        + [state] * 12
        + [sems] * 12
        + [pltpu.SemaphoreType.DMA((nh - 1,))] * 2,
        compiler_params=pltpu.CompilerParams(
            collective_id=0, has_side_effects=True, vmem_limit_bytes=60 * 1024 * 1024
        ),
    )(doc_lengths, queries, keys, values, gain.reshape(1, wide), cotangent)


def solution(mesh):
    placed = (
        P("seq", "head"),
        P("seq", "head"),
        P("seq", "head"),
        P("head"),
        P("seq", "head"),
        P(),
    )
    return jax.shard_map(
        functools.partial(on_device, mesh.shape["seq"], mesh.shape["head"]),
        mesh=mesh,
        in_specs=placed,
        out_specs=(P("seq", "head"), P("seq", "head"), P("seq", "head"), P("seq", "head")),
        check_vma=False,
    )
```

time: 583 us -> 125 us (0.21)
  waiting for transfers between devices: 294 us -> 0 us
  Pallas kernels: 0 us -> 115 us
  other arithmetic: 95.6 us -> 0 us
  local copies, waits for them, and re-layouts: 71.2 us -> 9.32 us
  matrix products: 55.8 us -> 0 us
  blocking collectives: 47.2 us -> 0 us
  between operations: 16.7 us -> 0.65 us
    all_gather x2 -> x0, waiting for transfers between devices: 294 us -> none  [carried_in(): pieces = jax.tree.map(lambda part: lax.all_gather(part, axis), value)]
    pallas_call x0 -> x1, Pallas kernels: none -> 115 us  [on_device(): pl.pallas_call(functools.partial(kernel, n, nh, doc_lengths.shape[0]), ou...]
    select_n x30 -> x0, other arithmetic: 83.4 us -> none  [step(): jnp.where(position < mine, new, old)]
    dot_general x12 -> x0, matrix products: 55.8 us -> none  [the longest x1 7.78 us: on_device(): jnp.einsum('hts,thk->shk', back_weights, query_row_list, preferred_elemen...]
    unnamed x1 -> x0, blocking collectives: 44.5 us -> none
    dynamic_slice x30 -> x0, local copies, waits for them, and re-layouts: 17.6 us -> none  [step(): longer = join(subtotal, jax.tree.map(lambda part: part[position], pieces))]
    reshape x4 -> x0, local copies, waits for them, and re-layouts: 17.6 us -> none  [the longest x1 5.46 us: on_device(): flat_out = output_rows.reshape(tokens, heads_here * DH)]
    unnamed x29 -> x10, local copies, waits for them, and re-layouts: 22.8 us -> 9.32 us
  transfers between devices with their start and end apart: 2 -> 0, of which waited for: 2 -> 0; matrix products, arithmetic and copies ran while one was open for 7% -> 0% of each run, Pallas kernels for 0% -> 0%
where the time goes in v1:
time: 125 us
  Pallas kernels  115 us (92%)
  local copies, waits for them, and re-layouts  9.32 us (7%)
    pallas_call x1, Pallas kernels, on_device(): pl.pallas_call(functools.partial(kernel, n, nh, doc_lengths.shape[0]), ou...  115 us
    unnamed x10, local copies, waits for them, and re-layouts  9.32 us

profile of v1, /device:TPU:0, one launch (start us, length us, event | category | flops | bytes accessed | tf_op | source)
XLA Modules:
  0.0 124.6 jit_solution(5704100331413952444)
XLA Ops:
  0.6 114.7 %shard_map.93 = (bf16[512,2048]{1,0:T(8,128)(2,1)}, bf16[512,2048]{1,0:T(8,128)(2,1)}, bf16[512,2048]{1,0:T(8,128)(2,1)}, bf16[512,2048]{1,0:T(8,128)(2,1)}) custom-call(s32[16]{0:T(128)} %lens.1, bf16[512,2048]{1,0:T(8,128)(2,1)} %q.1, bf16[512,2048]{1,0:T(8,128)(2,1)} %k.1, bf16[512,2048]{1,0:T(8,128)(2,1)} %v.1, f32[1,2048]{1,0:T(1,128)} %bitcast.1, ...), custom_call_target="tpu_custom_call" | custom-call | tf_op jit(solution)/shard_map/pallas_call | solution.py:355
  115.3 0.0 copy-start.2
  115.3 3.3 %copy.14 = bf16[512,2048]{1,0:T(8,128)(2,1)} copy(bf16[512,2048]{1,0:T(8,128)(2,1)} %get-tuple-element.8) | data formatting | bytes 4194304
  118.6 0.0 copy-done.2
  118.6 0.0 copy-start.1
  118.6 1.3 %copy.15 = bf16[512,2048]{1,0:T(8,128)(2,1)} copy(bf16[512,2048]{1,0:T(8,128)(2,1)S(1)} %copy-done.2) | data formatting | bytes 4194304
  119.9 1.0 copy-done.1
  121.0 0.0 copy-start
  121.0 1.3 %copy.16 = bf16[512,2048]{1,0:T(8,128)(2,1)} copy(bf16[512,2048]{1,0:T(8,128)(2,1)S(1)} %copy-done.1) | data formatting | bytes 4194304
  122.3 1.0 copy-done
  123.3 1.3 %copy.17 = bf16[512,2048]{1,0:T(8,128)(2,1)} copy(bf16[512,2048]{1,0:T(8,128)(2,1)S(1)} %copy-done) | data formatting | bytes 4194304
Async XLA Ops:
  115.3 3.3 %copy-start.2 = (bf16[512,2048]{1,0:T(8,128)(2,1)S(1)}, bf16[512,2048]{1,0:T(8,128)(2,1)}, u32[]{:S(2)}) copy-start(bf16[512,2048]{1,0:T(8,128)(2,1)} %get-tuple-element.9) | copy-start | bytes 6291460
  118.6 2.3 %copy-start.1 = (bf16[512,2048]{1,0:T(8,128)(2,1)S(1)}, bf16[512,2048]{1,0:T(8,128)(2,1)}, u32[]{:S(2)}) copy-start(bf16[512,2048]{1,0:T(8,128)(2,1)} %get-tuple-element.10) | copy-start | bytes 6291460
  121.0 2.3 %copy-start = (bf16[512,2048]{1,0:T(8,128)(2,1)S(1)}, bf16[512,2048]{1,0:T(8,128)(2,1)}, u32[]{:S(2)}) copy-start(bf16[512,2048]{1,0:T(8,128)(2,1)} %get-tuple-element.11) | copy-start | bytes 6291460

commit v2 on v1

--- a/solution.py
+++ b/solution.py
@@ -10,6 +10,8 @@
 DH = 128
 HEADS = 32
 QUAD = 4
+LAG = 3
+HOP = 2
 
 epsilon = 1e-05
 MESH = pl.DeviceIdType.MESH
@@ -39,16 +41,25 @@
 
 def kernel(
     n, nh, docs,
-    lens, q, k, v, gain, cot,
-    att, gq, gk, gv,
+    lens, qh, kh, vh, gain, coth,
+    atth, gqh, gkh, gvh,
+    q, k, v, cot, att, gq, gk, gv,
     wts, out, gks, grad, carr,
     vis, ment, mopen, mclose, mleave, part, peer,
     loc_f, pair_f, chain_f, rx_f, ry_f, rz_f,
     loc_b, pair_b, chain_b, rx_b, ry_b, rz_b,
     sx_f, sy_f, sz_f, tx_f, ty_f, tz_f,
     sx_b, sy_b, sz_b, tx_b, ty_b, tz_b,
-    sh, th,
+    sh, th, sin, satt, sgq, sgk, sgv,
 ):
+    load_q = pltpu.make_async_copy(qh, q, sin.at[0])
+    load_k = pltpu.make_async_copy(kh, k, sin.at[1])
+    load_v = pltpu.make_async_copy(vh, v, sin.at[2])
+    load_cot = pltpu.make_async_copy(coth, cot, sin.at[3])
+    load_k.start()
+    load_v.start()
+    load_q.start()
+    load_cot.start()
     tokens = q.shape[0]
     half = tokens // 2
     heads = q.shape[1] // DH
@@ -121,6 +132,10 @@
 
     def cols(h):
         return pl.ds(pl.multiple_of(h * DH, DH), DH)
+
+    def store(src, dst, sem, h):
+        c = cols(h)
+        return pltpu.make_async_copy(src.at[:, c], dst.at[:, c], sem.at[h])
 
     def send(src, dst, ss, rs, h, to):
         return pltpu.make_async_remote_copy(
@@ -214,7 +229,7 @@
 
     def slots(scan, inside, finish):
         def place_of(s):
-            return s - 1 - 2 * scan.place
+            return s - LAG - HOP * scan.place
 
         def chain_step(s):
             h = place_of(s)
@@ -226,22 +241,28 @@
         def main(s, carry):
             scan.xstage(s)
 
-            @pl.when(s > 0)
-            def _():
-                scan.ystage(s - 1)
+            @pl.when(s >= LAG)
+            def _():
+                scan.ystage(s - LAG)
 
             inside(s)
             chain_step(s)
             return carry
 
         lax.fori_loop(0, heads, main, 0)
-        scan.ystage(heads - 1)
 
         def tail(s, carry):
+            @pl.when(s < heads + LAG)
+            def _():
+                scan.ystage(s - LAG)
+
             chain_step(s)
             return carry
 
-        lax.fori_loop(heads, heads + 1 + 2 * (nz - 1), tail, 0)
+        lax.fori_loop(heads, heads + LAG + HOP * (nz - 1), tail, 0)
+
+    load_k.wait()
+    load_v.wait()
 
     def first(h, carry):
         c = cols(h)
@@ -284,6 +305,8 @@
         part[0] += o * o
         part[1] += (cot[:, c].astype(F32) * gain[:, c]) * o
 
+    load_q.wait()
+    load_cot.wait()
     slots(fwd, inside_f, finish_f)
 
     def swap(d):
@@ -313,6 +336,7 @@
         inv = part[0]
         gn = gain[:, c]
         att[:, c] = (o * inv * gn).astype(BF16)
+        store(att, atth, satt, h).start()
         g = ((cot[:, c].astype(F32) * gn - o * part[1]) * inv).astype(BF16)
         grad[:, c] = g
         loc_b[h] = tn(q[:, c] * mopen[...], g)
@@ -328,6 +352,7 @@
         entering = nt(grad[:, c] * ment[...], carr[h])
         gq[lo, c] = (nn(b0, k[lo, c]) + entering[lo]).astype(BF16)
         gq[hi, c] = (nn(b1, k[:, c]) + entering[hi]).astype(BF16)
+        store(gq, gqh, sgq, h).start()
         gks[lo, c] = tn(b0, q[lo, c]) + tn(b1[:, lo], q[hi, c])
         gks[hi, c] = tn(b1[:, hi], q[hi, c])
         w1 = wts[h, hi, :]
@@ -338,26 +363,45 @@
         c = cols(h)
         gk[:, c] = (gks[:, c] + nt(v[:, c] * mleave[...], low)).astype(BF16)
         gv[:, c] = (out[:, c] + nn(k[:, c] * mleave[...], low)).astype(BF16)
+        store(gk, gkh, sgk, h).start()
+        store(gv, gvh, sgv, h).start()
 
     slots(bwd, inside_b, finish_b)
     fwd.drain()
     bwd.drain()
+
+    def flush(h, carry):
+        store(att, atth, satt, h).wait()
+        store(gq, gqh, sgq, h).wait()
+        store(gk, gkh, sgk, h).wait()
+        store(gv, gvh, sgv, h).wait()
+        return carry
+
+    lax.fori_loop(0, heads, flush, 0)
+
+
+def move(*refs):
+    for src, dst in zip(refs[:4], refs[4:]):
+        dst[...] = src[...]
 
 
 def on_device(n, nh, queries, keys, values, gain, cotangent, doc_lengths):
     tokens, wide = queries.shape
     heads = wide // DH
     vmem = pl.BlockSpec(memory_space=pltpu.VMEM)
+    hbm = pl.BlockSpec(memory_space=pl.ANY)
+    block = pl.BlockSpec((tokens // 8, wide), lambda i: (i, 0))
     state = pltpu.VMEM((heads, DH, DH), F32)
     sems = pltpu.SemaphoreType.DMA((heads,))
     low = pltpu.VMEM((tokens, DH), BF16)
     shape = jax.ShapeDtypeStruct((tokens, wide), BF16)
-    return pl.pallas_call(
+    results = pl.pallas_call(
         functools.partial(kernel, n, nh, doc_lengths.shape[0]),
         out_shape=(shape,) * 4,
-        in_specs=[pl.BlockSpec(memory_space=pltpu.SMEM)] + [vmem] * 5,
-        out_specs=(vmem,) * 4,
-        scratch_shapes=[
+        in_specs=[pl.BlockSpec(memory_space=pltpu.SMEM)] + [hbm] * 3 + [vmem, hbm],
+        out_specs=(hbm,) * 4,
+        scratch_shapes=[pltpu.VMEM((tokens, wide), BF16)] * 8
+        + [
             pltpu.VMEM((heads, tokens, tokens), BF16),
             pltpu.VMEM((tokens, wide), F32),
             pltpu.VMEM((tokens, wide), F32),
@@ -370,11 +414,20 @@
         ]
         + [state] * 12
         + [sems] * 12
-        + [pltpu.SemaphoreType.DMA((nh - 1,))] * 2,
+        + [pltpu.SemaphoreType.DMA((nh - 1,))] * 2
+        + [pltpu.SemaphoreType.DMA((4,))]
+        + [sems] * 4,
         compiler_params=pltpu.CompilerParams(
             collective_id=0, has_side_effects=True, vmem_limit_bytes=60 * 1024 * 1024
         ),
     )(doc_lengths, queries, keys, values, gain.reshape(1, wide), cotangent)
+    return pl.pallas_call(
+        move,
+        grid=(8,),
+        out_shape=(shape,) * 4,
+        in_specs=[block] * 4,
+        out_specs=(block,) * 4,
+    )(*results)
 
 
 def solution(mesh):

time: 125 us -> 100 us (0.80)
  Pallas kernels: 115 us -> 99.4 us
  local copies, waits for them, and re-layouts: 9.32 us -> 0 us
    pallas_call x1, Pallas kernels: 115 us -> 90.6 us  [on_device(): pl.pallas_call(functools.partial(kernel, n, nh, doc_lengths.shape[0]), ou...]
    unnamed x10 -> x0, local copies, waits for them, and re-layouts: 9.32 us -> none
    pallas_call x0 -> x1, Pallas kernels: none -> 8.82 us  [on_device(): pl.pallas_call(move, grid=(8,), out_shape=(shape,) * 4, in_specs=[block]...]
where the time goes in v2:
time: 100 us
  Pallas kernels  99.4 us (99%)
    pallas_call x1, Pallas kernels, on_device(): pl.pallas_call(functools.partial(kernel, n, nh, doc_lengths.shape[0]), ou...  90.6 us
    pallas_call x1, Pallas kernels, on_device(): pl.pallas_call(move, grid=(8,), out_shape=(shape,) * 4, in_specs=[block]...  8.82 us

profile of v2, /device:TPU:0, one launch (start us, length us, event | category | flops | bytes accessed | tf_op | source)
XLA Modules:
  0.0 100.1 jit_solution(7415610697122867177)
XLA Ops:
  0.6 90.6 %shard_map.93 = (bf16[512,2048]{1,0:T(8,128)(2,1)}, bf16[512,2048]{1,0:T(8,128)(2,1)}, bf16[512,2048]{1,0:T(8,128)(2,1)}, bf16[512,2048]{1,0:T(8,128)(2,1)}) custom-call(s32[16]{0:T(128)} %lens.1, bf16[512,2048]{1,0:T(8,128)(2,1)} %qh.1, bf16[512,2048]{1,0:T(8,128)(2,1)} %kh.1, bf16[512,2048]{1,0:T(8,128)(2,1)} %vh.1, f32[1,2048]{1,0:T(1,128)} %bitcast.1, ...), custom_call_target="tpu_custom_call" | custom-call | tf_op jit(solution)/shard_map/pallas_call | solution.py:398
  91.2 8.8 %shard_map.94 = (bf16[512,2048]{1,0:T(8,128)(2,1)}, bf16[512,2048]{1,0:T(8,128)(2,1)}, bf16[512,2048]{1,0:T(8,128)(2,1)}, bf16[512,2048]{1,0:T(8,128)(2,1)}) custom-call(bf16[512,2048]{1,0:T(8,128)(2,1)} %get-tuple-element.8.refs_0_, bf16[512,2048]{1,0:T(8,128)(2,1)} %get-tuple-element.9.refs_1_, bf16[512,2048]{1,0:T(8,128)(2,1)} %get-tuple-element.10.refs_2_, ...), custom_call_target="tpu_custom_call" | custom-call | tf_op jit(solution)/shard_map/pallas_call | solution.py:424

commit v3 on v2

--- a/solution.py
+++ b/solution.py
@@ -380,24 +380,18 @@
     lax.fori_loop(0, heads, flush, 0)
 
 
-def move(*refs):
-    for src, dst in zip(refs[:4], refs[4:]):
-        dst[...] = src[...]
-
-
 def on_device(n, nh, queries, keys, values, gain, cotangent, doc_lengths):
     tokens, wide = queries.shape
     heads = wide // DH
     vmem = pl.BlockSpec(memory_space=pltpu.VMEM)
     hbm = pl.BlockSpec(memory_space=pl.ANY)
-    block = pl.BlockSpec((tokens // 8, wide), lambda i: (i, 0))
     state = pltpu.VMEM((heads, DH, DH), F32)
     sems = pltpu.SemaphoreType.DMA((heads,))
     low = pltpu.VMEM((tokens, DH), BF16)
     shape = jax.ShapeDtypeStruct((tokens, wide), BF16)
     results = pl.pallas_call(
         functools.partial(kernel, n, nh, doc_lengths.shape[0]),
-        out_shape=(shape,) * 4,
+        out_shape=(pltpu.VMEM((tokens, wide), BF16),) * 4,
         in_specs=[pl.BlockSpec(memory_space=pltpu.SMEM)] + [hbm] * 3 + [vmem, hbm],
         out_specs=(hbm,) * 4,
         scratch_shapes=[pltpu.VMEM((tokens, wide), BF16)] * 8
@@ -418,16 +412,10 @@
         + [pltpu.SemaphoreType.DMA((4,))]
         + [sems] * 4,
         compiler_params=pltpu.CompilerParams(
-            collective_id=0, has_side_effects=True, vmem_limit_bytes=60 * 1024 * 1024
+            collective_id=0, has_side_effects=True, vmem_limit_bytes=51 * 1024 * 1024
         ),
     )(doc_lengths, queries, keys, values, gain.reshape(1, wide), cotangent)
-    return pl.pallas_call(
-        move,
-        grid=(8,),
-        out_shape=(shape,) * 4,
-        in_specs=[block] * 4,
-        out_specs=(block,) * 4,
-    )(*results)
+    return results
 
 
 def solution(mesh):

time: 100 us -> 98.6 us (0.986)
  Pallas kernels: 99.4 us -> 92.4 us
  local copies, waits for them, and re-layouts: 0 us -> 5.28 us
    pallas_call x1 -> x0, Pallas kernels: 8.82 us -> none  [on_device(): pl.pallas_call(move, grid=(8,), out_shape=(shape,) * 4, in_specs=[block]...]
    unnamed x0 -> x4, local copies, waits for them, and re-layouts: none -> 5.28 us
    pallas_call x1, Pallas kernels: 90.6 us -> 92.4 us  [on_device(): pl.pallas_call(functools.partial(kernel, n, nh, doc_lengths.shape[0]), ou...]
where the time goes in v3:
time: 98.6 us; the launch traced here: 98.4 us
  Pallas kernels  92.4 us (94%)
  local copies, waits for them, and re-layouts  5.28 us (5%)
    pallas_call x1, Pallas kernels, on_device(): pl.pallas_call(functools.partial(kernel, n, nh, doc_lengths.shape[0]), ou...  92.4 us
    unnamed x4, local copies, waits for them, and re-layouts  5.28 us

profile of v3, /device:TPU:0, one launch (start us, length us, event | category | flops | bytes accessed | tf_op | source)
XLA Modules:
  0.0 98.4 jit_solution(17041371564457451198)
XLA Ops:
  0.6 92.4 %shard_map.93 = (bf16[512,2048]{1,0:T(8,128)(2,1)S(1)}, bf16[512,2048]{1,0:T(8,128)(2,1)S(1)}, bf16[512,2048]{1,0:T(8,128)(2,1)S(1)}, bf16[512,2048]{1,0:T(8,128)(2,1)S(1)}) custom-call(s32[16]{0:T(128)} %lens.1, bf16[512,2048]{1,0:T(8,128)(2,1)} %qh.1, bf16[512,2048]{1,0:T(8,128)(2,1)} %kh.1, bf16[512,2048]{1,0:T(8,128)(2,1)} %vh.1, f32[1,2048]{1,0:T(1,128)} %bitcast.1, ...), custom_call_target="tpu_custom_call" | custom-call | tf_op jit(solution)/shard_map/pallas_call | solution.py:392
  93.1 1.3 %copy.14 = bf16[512,2048]{1,0:T(8,128)(2,1)} copy(bf16[512,2048]{1,0:T(8,128)(2,1)S(1)} %get-tuple-element.4) | data formatting | bytes 4194304
  94.4 1.3 %copy.15 = bf16[512,2048]{1,0:T(8,128)(2,1)} copy(bf16[512,2048]{1,0:T(8,128)(2,1)S(1)} %get-tuple-element.5) | data formatting | bytes 4194304
  95.7 1.3 %copy.16 = bf16[512,2048]{1,0:T(8,128)(2,1)} copy(bf16[512,2048]{1,0:T(8,128)(2,1)S(1)} %get-tuple-element.6) | data formatting | bytes 4194304
  97.0 1.3 %copy.17 = bf16[512,2048]{1,0:T(8,128)(2,1)} copy(bf16[512,2048]{1,0:T(8,128)(2,1)S(1)} %get-tuple-element.7) | data formatting | bytes 4194304
